TPU v7x, 256 devices: a whole 4x4x8 slice. The times are simulated.
256 devices in a mesh: sub: 16 (over z, core), row: 16 (over y, x).
Axes of the slice: x: 4, y: 4, z: 8, core: 2. Of those that a mesh axis runs over, the one named last changes fastest.
Arguments:
- modes: float32 [196608, 64], P(('sub', 'row')), may hold values from -6 to 6
- search: float32 [196608, 64], P(('sub', 'row')), may hold values from -6 to 6
- precond: float32 [196608], P(('sub', 'row')), may hold values from 0.05 to 0.25
- in_row: int32 [16, 16, 96], P('sub', 'row'), may hold values from 0 to 11, as said below
- in_col: int32 [16, 16, 96], P('sub', 'row'), may hold values from 0 to 191, as said below
- in_val: bfloat16 [16, 16, 96, 64, 64], P('sub', 'row'), as said below
- bnd_rows: int32 [16, 16, 3], P('sub', 'row'), may hold values from 0 to 11, as said below
- if_row: int32 [16, 16, 12], P('sub', 'row'), may hold values from 0 to 11, as said below
- if_src: int32 [16, 16, 12], P('sub', 'row'), may hold values from 0 to 47, as said below
- if_val: bfloat16 [16, 16, 12, 64, 64], P('sub', 'row')
Outputs:
- modes_out: float32 [196608, 64], P(('sub', 'row'))
- search_out: float32 [196608, 64], P(('sub', 'row'))
Inputs may be any that keep to these rules, and one draw needn't show every extreme that they name: `in_row`: entry k < 12 is k; each later group of 12 entries names each of the device's block-rows once. `in_col`: entry k < 12 is r * 12 + k on device (s, r); in each later group of 12 entries the devices of a subdomain together name each of its 192 block-rows once, and no entry names its own block-row. `in_val`: the first 12 blocks of every device are symmetric; the operator A is symmetric positive definite. `bnd_rows`: distinct within a device. `if_row`: each of the device's 12 block-rows once. `if_src`: t * 3 + q with t never the device's own subdomain; among the devices with one index of row, each boundary slot of each subdomain is named exactly 4 times.
All inputs are finite; a program needn't handle non-finite values.
Results may differ from a plain program's by a relative error of at most 0.0006.
Values may be sent and summed in bfloat16 or wider, within the bound.
A program may use at most 128 MiB of HBM per device.

v0:
```python
import jax
import jax.numpy as jnp
from jax import lax
from jax.sharding import PartitionSpec as P

KB = 64
LB = 12
ITERS = 2
IFR = 3
precise_mode = lax.Precision.HIGHEST


def gram_product(left, right):
    return jnp.dot(left.T, right, precision=precise_mode, preferred_element_type=jnp.float32)


def full_dot(left, right):
    return jnp.dot(left, right, precision=precise_mode, preferred_element_type=jnp.float32)


def chol_solve(matrix, rhs):
    factor = jnp.linalg.cholesky(matrix)
    halfway = lax.linalg.triangular_solve(factor, rhs, left_side=True, lower=True)
    return lax.linalg.triangular_solve(
        factor, halfway, left_side=True, lower=True, transpose_a=True
    )


def rescale(factor, moved):
    return lax.linalg.triangular_solve(factor, moved, left_side=False, lower=True, transpose_a=True)


def project(current, image_x):
    return lax.psum(
        (gram_product(current, current), gram_product(current, image_x)), ("sub", "row")
    )


def apply_blocks(vector, blocks):
    rows_here, cols_here, vals_here, bnd_here, face_rows, face_src, face_vals = blocks
    width = vector.shape[1]
    mine = vector.reshape(LB, KB, width)
    local_ids = jnp.arange(LB, dtype=jnp.int32)
    position = lax.axis_index("row")
    group = lax.all_gather(vector, "row", axis=0, tiled=True).reshape(-1, KB, width)
    forward = jnp.einsum("kij,kjw->kiw", vals_here, group[cols_here], precision=precise_mode)
    select = (rows_here[:, None] == local_ids[None, :]).astype(jnp.float32)
    result = jnp.einsum("ka,kiw->aiw", select, forward, precision=precise_mode)
    backward = jnp.einsum("kji,kjw->kiw", vals_here, mine[rows_here], precision=precise_mode)
    keeper = (cols_here != position * LB + rows_here).astype(jnp.float32)
    backward = backward * keeper[:, None, None]
    wanted = jnp.arange(LB * KB * lax.axis_size("row") // KB, dtype=jnp.int32)
    chosen = (cols_here[None, :] == wanted[:, None]).astype(jnp.float32)
    returned = lax.psum_scatter(
        jnp.einsum("bk,kiw->biw", chosen, backward, precision=precise_mode).reshape(
            LB * KB * lax.axis_size("row"), width
        ),
        "row",
        scatter_dimension=0,
        tiled=True,
    )
    result = result + returned.reshape(LB, KB, width)
    boundary = mine[bnd_here].reshape(-1, width)
    remote = lax.all_gather(boundary, "sub", axis=0, tiled=True).reshape(-1, KB, width)
    forward = jnp.einsum("kij,kjw->kiw", face_vals, remote[face_src], precision=precise_mode)
    face_select = (face_rows[:, None] == local_ids[None, :]).astype(jnp.float32)
    result = result + jnp.einsum("ka,kiw->aiw", face_select, forward, precision=precise_mode)
    backward = jnp.einsum("kji,kjw->kiw", face_vals, mine[face_rows], precision=precise_mode)
    wanted = jnp.arange(IFR * KB * lax.axis_size("sub") // KB, dtype=jnp.int32)
    chosen = (face_src[None, :] == wanted[:, None]).astype(jnp.float32)
    landed = lax.psum_scatter(
        jnp.einsum("bk,kiw->biw", chosen, backward, precision=precise_mode).reshape(
            IFR * KB * lax.axis_size("sub"), width
        ),
        "sub",
        scatter_dimension=0,
        tiled=True,
    ).reshape(IFR, KB, width)
    placed = (bnd_here[:, None] == local_ids[None, :]).astype(jnp.float32)
    result = result + jnp.einsum("qa,qiw->aiw", placed, landed, precision=precise_mode)
    return result.reshape(LB * KB, width)


def local(modes, search, precond, in_row, in_col, in_val, bnd_rows, if_row, if_src, if_val):
    blocks = (
        in_row[0, 0],
        in_col[0, 0],
        in_val[0, 0].astype(jnp.float32),
        bnd_rows[0, 0],
        if_row[0, 0],
        if_src[0, 0],
        if_val[0, 0].astype(jnp.float32),
    )
    total_rows = modes.shape[0] * lax.axis_size("sub") * lax.axis_size("row")
    nmode = modes.shape[1]
    images = apply_blocks(jnp.concatenate([modes, search], 1), blocks)
    current, direction = (modes, search)
    image_x, image_p = (images[:, :nmode], images[:, nmode:])
    for sweep in range(ITERS):
        correlation, energy = project(current, image_x)
        ritz = chol_solve(correlation, energy)
        residue = image_x - full_dot(current, ritz)
        update = precond[:, None] * residue
        image_w = apply_blocks(update, blocks)
        basis = jnp.concatenate([update, direction], 1)
        image_b = jnp.concatenate([image_w, image_p], 1)
        coupled, driving = lax.psum(
            (gram_product(basis, image_b), gram_product(basis, image_x)), ("sub", "row")
        )
        coeffs = -chol_solve(coupled, driving)
        step_x = full_dot(basis, coeffs)
        step_a = full_dot(image_b, coeffs)
        moved = current + step_x
        moved_image = image_x + step_a
        lengths = lax.psum(gram_product(moved, moved), ("sub", "row"))
        factor = jnp.linalg.cholesky(lengths / total_rows)
        current = rescale(factor, moved)
        image_x = rescale(factor, moved_image)
        direction = rescale(factor, step_x)
        image_p = rescale(factor, step_a)
    return (current, direction)


def solution(mesh):
    return jax.shard_map(
        local,
        mesh=mesh,
        in_specs=(
            P(("sub", "row"), None),
            P(("sub", "row"), None),
            P(("sub", "row")),
            P("sub", "row", None),
            P("sub", "row", None),
            P("sub", "row", None, None, None),
            P("sub", "row", None),
            P("sub", "row", None),
            P("sub", "row", None),
            P("sub", "row", None, None, None),
        ),
        out_specs=(P(("sub", "row"), None), P(("sub", "row"), None)),
        check_vma=False,
    )
```

profile of v0, /device:TPU:1, one launch (start us, length us, event | category | flops | bytes accessed | tf_op | source)
XLA Modules:
  0.0 1590.2 jit_solution(9537704448237477838)
XLA Ops:
  41.8 13.2 all-gather.9.cloned.1.call-done
  57.4 53.8 %reduce-scatter.13.cloned.1.call-done = f32[192,128]{1,0:T(8,128)} async-done(((f32[3072,128]{1,0:T(8,128)}), f32[192,128]{1,0:T(8,128)}) %reduce-scatter.13.cloned.1.call-update) | async-done | bytes 98320 | tf_op jit(solution)/shard_map/reduce_scatter | solution.py:71
  112.6 69.1 %all-gather.7.cloned.1.call-done = f32[12288,128]{1,0:T(8,128)} async-done(((f32[768,128]{1,0:T(8,128)}), f32[12288,128]{1,0:T(8,128)}) %all-gather.7.cloned.1.call-update) | async-done | bytes 6291472 | tf_op jit(solution)/shard_map/all_gather | solution.py:45
  192.2 78.6 %reduce-scatter.11.cloned.1.call-done = f32[768,128]{1,0:T(8,128)} async-done(((f32[12288,128]{1,0:T(8,128)}), f32[768,128]{1,0:T(8,128)}) %reduce-scatter.11.cloned.1.call-update) | async-done | bytes 393232 | tf_op jit(solution)/shard_map/reduce_scatter | solution.py:54
  277.3 76.9 %all-reduce.1 = (f32[64,64]{0,1:T(8,128)S(1)}, f32[64,64]{0,1:T(8,128)S(1)}) all-reduce(f32[64,64]{0,1:T(8,128)S(1)} %convolution_bitcast_fusion.16, f32[64,64]{0,1:T(8,128)} %fusion.130), channel_id=1, replica_groups=mesh['sub'=16,'row'=16] {'sub','row'}, use_global_device_ids=true, to_apply=%region_5.0 | all-reduce | flops 8192 | bytes 65536 | tf_op jit(solution)/shard_map/psum | solution.py:34
  381.2 6.5 multiply_bitcast_fusion.1
  411.0 21.9 %all-gather = f32[16,192,64]{1,2,0:T(8,128)} all-gather(f32[1,192,64]{1,2,0:T(8,128)S(1)} %copy.168), channel_id=1, replica_groups=mesh['sub'=16,'row'=16] {'sub'}, dimensions={0}, use_global_device_ids=true | all-gather | bytes 835584 | tf_op jit(solution)/shard_map/all_gather | solution.py:64
  441.7 45.4 %all-gather.11.cloned.1.call-done = f32[12288,64]{0,1:T(8,128)} async-done(((f32[768,64]{0,1:T(8,128)}), f32[12288,64]{0,1:T(8,128)}) %all-gather.11.cloned.1.call-update) | async-done | bytes 3145744 | tf_op jit(solution)/shard_map/all_gather | solution.py:45
  509.1 60.1 %reduce-scatter.15.cloned.1.call-done = f32[768,64]{0,1:T(8,128)} async-done(((f32[12288,64]{0,1:T(8,128)}), f32[768,64]{0,1:T(8,128)}) %reduce-scatter.15.cloned.1.call-update) | async-done | bytes 196624 | tf_op jit(solution)/shard_map/reduce_scatter | solution.py:54
  582.2 77.9 %psum.73 = f32[128,64]{0,1:T(8,128)S(1)} all-reduce(f32[128,64]{0,1:T(8,128)} %fusion.27), channel_id=1, replica_groups=mesh['sub'=16,'row'=16] {'sub','row'}, use_global_device_ids=true, to_apply=%region_11.16 | all-reduce | flops 8192 | bytes 65536 | tf_op jit(solution)/shard_map/psum | solution.py:107
  660.1 160.0 %all-reduce.5.cloned.1.call-done = f32[128,128]{0,1:T(8,128)} async-done(((f32[128,128]{0,1:T(8,128)}), f32[128,128]{0,1:T(8,128)}) %all-reduce.5.cloned.1.call-update) | async-done | bytes 65552 | tf_op jit(solution)/shard_map/psum | solution.py:107
  821.9 11.7 cholesky.127
  835.0 9.8 custom-call.31
  847.9 74.6 %psum.74 = f32[64,64]{0,1:T(8,128)S(1)} all-reduce(f32[64,64]{0,1:T(8,128)S(1)} %fusion.131), channel_id=1, replica_groups=mesh['sub'=16,'row'=16] {'sub','row'}, use_global_device_ids=true, to_apply=%region_12.19 | all-reduce | flops 4096 | bytes 32768 | tf_op jit(solution)/shard_map/psum | solution.py:115
  937.0 74.2 %all-reduce = (f32[64,64]{1,0:T(8,128)S(1)}, f32[64,64]{0,1:T(8,128)S(1)}) all-reduce(f32[64,64]{1,0:T(8,128)S(1)} %fusion.133, f32[64,64]{0,1:T(8,128)S(1)} %fusion.132), channel_id=1, replica_groups=mesh['sub'=16,'row'=16] {'sub','row'}, use_global_device_ids=true, to_apply=%region_14.22 | all-reduce | flops 8192 | bytes 65536 | tf_op jit(solution)/shard_map/psum | solution.py:34
  1034.0 6.6 multiply_bitcast_fusion
  1063.8 19.7 %all-gather.1 = f32[16,192,64]{1,2,0:T(8,128)S(1)} all-gather(f32[1,192,64]{1,2,0:T(8,128)S(1)} %copy.198), channel_id=1, replica_groups=mesh['sub'=16,'row'=16] {'sub'}, dimensions={0}, use_global_device_ids=true | all-gather | bytes 835584 | tf_op jit(solution)/shard_map/all_gather | solution.py:64
  1091.1 47.1 %all-gather.13.cloned.1.call-done = f32[12288,64]{0,1:T(8,128)} async-done(((f32[768,64]{0,1:T(8,128)}), f32[12288,64]{0,1:T(8,128)}) %all-gather.13.cloned.1.call-update) | async-done | bytes 3145744 | tf_op jit(solution)/shard_map/all_gather | solution.py:45
  1160.1 60.5 %reduce-scatter.17.cloned.1.call-done = f32[768,64]{0,1:T(8,128)} async-done(((f32[12288,64]{0,1:T(8,128)}), f32[768,64]{0,1:T(8,128)}) %reduce-scatter.17.cloned.1.call-update) | async-done | bytes 196624 | tf_op jit(solution)/shard_map/reduce_scatter | solution.py:54
  1229.7 77.7 %psum.78 = f32[128,64]{0,1:T(8,128)S(1)} all-reduce(f32[128,64]{0,1:T(8,128)S(1)} %fusion.25), channel_id=1, replica_groups=mesh['sub'=16,'row'=16] {'sub','row'}, use_global_device_ids=true, to_apply=%region_18.26 | all-reduce | flops 8192 | bytes 65536 | tf_op jit(solution)/shard_map/psum | solution.py:107
  1307.4 161.1 %all-reduce.7.cloned.1.call-done = f32[128,128]{0,1:T(8,128)} async-done(((f32[128,128]{0,1:T(8,128)}), f32[128,128]{0,1:T(8,128)}) %all-reduce.7.cloned.1.call-update) | async-done | bytes 65552 | tf_op jit(solution)/shard_map/psum | solution.py:107
  1470.3 11.7 cholesky.160
  1483.3 9.8 custom-call.39
  1494.3 74.6 %psum.79 = f32[64,64]{0,1:T(8,128)S(1)} all-reduce(f32[64,64]{0,1:T(8,128)S(1)} %fusion.134), channel_id=1, replica_groups=mesh['sub'=16,'row'=16] {'sub','row'}, use_global_device_ids=true, to_apply=%region_19.27 | all-reduce | flops 4096 | bytes 32768 | tf_op jit(solution)/shard_map/psum | solution.py:115
  (245 shorter events, 272.3 us)
Async XLA Ops:
  7.2 47.9 %all-gather.9.cloned.1.call-start = ((), (), s32[]{:S(2)}) async-start(), calls=%async_computation.8 | async-start | bytes 1671168 | tf_op jit(solution)/shard_map/all_gather | solution.py:64
  11.5 99.6 %reduce-scatter.13.cloned.1.call-start = ((), (), s32[]{:S(2)}) async-start(), calls=%async_computation.9 | async-start | bytes 1671168 | tf_op jit(solution)/shard_map/reduce_scatter | solution.py:71
  15.9 165.8 %all-gather.7.cloned.1.call-start = ((), (), s32[]{:S(2)}) async-start(), calls=%async_computation.6 | async-start | bytes 6684672 | tf_op jit(solution)/shard_map/all_gather | solution.py:45
  16.6 254.2 %reduce-scatter.11.cloned.1.call-start = ((), (), s32[]{:S(2)}) async-start(), calls=%async_computation.7 | async-start | bytes 6684672 | tf_op jit(solution)/shard_map/reduce_scatter | solution.py:54
  37.3 73.9 %copy-start.29 = (s32[1,1,3]{2,1,0:T(1,128)S(1)}, s32[1,1,3]{2,1,0:T(1,128)}, u32[]{:S(2)}) copy-start(s32[1,1,3]{2,1,0:T(1,128)} %param.28) | copy-start | bytes 40
  37.3 402.2 %reduce-scatter.19.cloned.1.call-start = ((), (), s32[]{:S(2)}) async-start(), calls=%async_computation.16 | async-start | bytes 1671168 | tf_op jit(solution)/shard_map/reduce_scatter | solution.py:71
  40.8 146.0 %copy-start.20 = (s32[1024]{0:T(1024)}, s32[1024]{0:T(1024)S(1)}, u32[]{:S(2)}) copy-start(s32[1024]{0:T(1024)S(1)} %pad_clamp_fusion.4) | copy-start | bytes 12292
  40.9 14.2 copy-start.23
  192.2 83.4 %copy-start.26 = (s32[1,1,12]{2,1,0:T(1,128)S(1)}, s32[1,1,12]{2,1,0:T(1,128)}, u32[]{:S(2)}) copy-start(s32[1,1,12]{2,1,0:T(1,128)} %param.29) | copy-start | bytes 148
  275.6 92.0 %copy-start.17 = (f32[768]{0:T(1024)S(1)}, f32[768]{0:T(1024)}, u32[]{:S(2)}) copy-start(f32[768]{0:T(1024)} %param.24) | copy-start | bytes 9220
  367.6 10.2 copy-start.13
  377.8 109.3 %all-gather.11.cloned.1.call-start = ((), (), s32[]{:S(2)}) async-start(), calls=%async_computation.10 | async-start | bytes 3342336 | tf_op jit(solution)/shard_map/all_gather | solution.py:45
  378.4 190.8 %reduce-scatter.15.cloned.1.call-start = ((), (), s32[]{:S(2)}) async-start(), calls=%async_computation.11 | async-start | bytes 3342336 | tf_op jit(solution)/shard_map/reduce_scatter | solution.py:54
  410.2 410.0 %all-reduce.5.cloned.1.call-start = ((), (), s32[]{:S(2)}) async-start(), calls=%async_computation.12 | async-start | bytes 131072 | tf_op jit(solution)/shard_map/psum | solution.py:107
  509.0 68.4 %copy-start.27 = (s32[1,1,12]{2,1,0:T(1,128)S(1)}, s32[1,1,12]{2,1,0:T(1,128)}, u32[]{:S(2)}) copy-start(s32[1,1,12]{2,1,0:T(1,128)} %param.29) | copy-start | bytes 148
  580.8 508.0 %reduce-scatter.21.cloned.1.call-start = ((), (), s32[]{:S(2)}) async-start(), calls=%async_computation.17 | async-start | bytes 1671168 | tf_op jit(solution)/shard_map/reduce_scatter | solution.py:71
  847.6 178.0 %copy-start.25 = (s32[1,1,12]{2,1,0:T(1,128)S(1)}, s32[1,1,12]{2,1,0:T(1,128)}, u32[]{:S(2)}) copy-start(s32[1,1,12]{2,1,0:T(1,128)} %param.30) | copy-start | bytes 148
  936.4 87.8 %copy-start.9 = (f32[768,64]{0,1:T(8,128)}, f32[768,64]{0,1:T(8,128)S(1)}, u32[]{:S(2)}) copy-start(f32[768,64]{0,1:T(8,128)S(1)} %convolution_bitcast_fusion.13) | copy-start | bytes 589828
  1030.8 107.3 %all-gather.13.cloned.1.call-start = ((), (), s32[]{:S(2)}) async-start(), calls=%async_computation.13 | async-start | bytes 3342336 | tf_op jit(solution)/shard_map/all_gather | solution.py:45
  1031.4 189.3 %reduce-scatter.17.cloned.1.call-start = ((), (), s32[]{:S(2)}) async-start(), calls=%async_computation.14 | async-start | bytes 3342336 | tf_op jit(solution)/shard_map/reduce_scatter | solution.py:54
  1063.0 405.5 %all-reduce.7.cloned.1.call-start = ((), (), s32[]{:S(2)}) async-start(), calls=%async_computation.15 | async-start | bytes 131072 | tf_op jit(solution)/shard_map/psum | solution.py:107
  1063.8 24.2 %copy-start.14 = (f32[768,64]{0,1:T(8,128)S(1)}, f32[768,64]{0,1:T(8,128)}, u32[]{:S(2)}) copy-start(f32[768,64]{0,1:T(8,128)} %fusion.42) | copy-start | bytes 589828
  1160.1 67.0 %copy-start.12 = (f32[12,64,64]{2,0,1:T(8,128)S(1)}, f32[12,64,64]{2,0,1:T(8,128)}, u32[]{:S(2)}) copy-start(f32[12,64,64]{2,0,1:T(8,128)} %fusion.36) | copy-start | bytes 589828
  1160.1 67.0 %copy-start.28 = (s32[1,1,12]{2,1,0:T(1,128)S(1)}, s32[1,1,12]{2,1,0:T(1,128)}, u32[]{:S(2)}) copy-start(s32[1,1,12]{2,1,0:T(1,128)} %param.29) | copy-start | bytes 148
  (19 other events, 90.9 us)
Sparse Core Ops, SparseCore 0:
  11.7 43.3 all-gather.8
  57.6 53.5 reduce-scatter.12
  113.9 67.7 all-gather.6
  185.7 85.0 reduce-scatter.10
  377.9 52.2 reduce-scatter.18
  433.1 53.9 all-gather.10
  490.7 78.4 reduce-scatter.14
  580.9 239.1 all-reduce.4
  1030.9 50.4 reduce-scatter.20
  1084.0 54.0 all-gather.12
  1142.2 78.3 reduce-scatter.16
  1229.3 239.1 all-reduce.6
where the time goes:
time: 1590 us
  waiting for transfers between devices  751 us (47%)
  blocking collectives  497 us (31%)
  local copies, waits for them, and re-layouts  128 us (8%)
  matrix products  100 us (6%)
  other arithmetic  97.2 us (6%)
    psum x2, waiting for transfers between devices, local(): lax.psum((gram_product(basis, image_b), gram_product(basis, image_x)), ('...  321 us
    reduce_scatter x6, waiting for transfers between devices, apply_blocks(): lax.psum_scatter(jnp.einsum('bk,kiw->biw', chosen, backward, precision=pr...  253 us
    all_gather x3, waiting for transfers between devices, apply_blocks(): lax.all_gather(vector, 'row', axis=0, tiled=True).reshape(-1, KB, width)  162 us
    psum x2, blocking collectives, local(): lax.psum((gram_product(basis, image_b), gram_product(basis, image_x)), ('...  156 us
    psum x2, blocking collectives, project(): lax.psum((gram_product(current, current), gram_product(current, image_x))...  151 us
    psum x2, blocking collectives, local(): lengths = lax.psum(gram_product(moved, moved), ('sub', 'row'))  149 us
    all_gather x2, blocking collectives, apply_blocks(): lax.all_gather(boundary, 'sub', axis=0, tiled=True).reshape(-1, KB, width)  41.6 us
    another operation x12, other arithmetic, chol_solve(): factor = jnp.linalg.cholesky(matrix)  37.8 us
  transfers between devices with their start and end apart: 12, of which 10 were waited for; matrix products, arithmetic and copies ran while one was open for 11% of the time, Pallas kernels for 0%

commit v1 on v0

--- a/solution.py
+++ b/solution.py
@@ -105,7 +105,7 @@
         basis = jnp.concatenate([update, direction], 1)
         image_b = jnp.concatenate([image_w, image_p], 1)
         coupled, driving = lax.psum(
-            (gram_product(basis, image_b), gram_product(basis, image_x)), ("sub", "row")
+            lax.psum((gram_product(basis, image_b), gram_product(basis, image_x)), "row"), "sub"
         )
         coeffs = -chol_solve(coupled, driving)
         step_x = full_dot(basis, coeffs)

time: 1590 us -> 1510 us (0.950)
  waiting for transfers between devices: 751 us -> 608 us
  blocking collectives: 497 us -> 553 us
    psum x2 -> x4, waiting for transfers between devices: 321 us -> 177 us  [the longest x2 114 us: local(): lax.psum(lax.psum((gram_product(basis, image_b), gram_product(basis, imag...]
    psum x2 -> x4, blocking collectives: 156 us -> 207 us  [the longest x2 116 us: local(): lax.psum((gram_product(basis, image_b), gram_product(basis, image_x)), 'r...]
  transfers between devices with their start and end apart: 12 -> 14, of which waited for: 10 -> 12; matrix products, arithmetic and copies ran while one was open for 11% -> 11% of each run, Pallas kernels for 0% -> 0%
where the time goes in v1:
time: 1510 us; the launch traced here: 1500 us
  waiting for transfers between devices  608 us (40%)
  blocking collectives  553 us (37%)
  local copies, waits for them, and re-layouts  128 us (8%)
  matrix products  99.9 us (7%)
  other arithmetic  97.2 us (6%)
  between operations  15.1 us (1%)
    reduce_scatter x6, waiting for transfers between devices, apply_blocks(): lax.psum_scatter(jnp.einsum('bk,kiw->biw', chosen, backward, precision=pr...  253 us
    all_gather x3, waiting for transfers between devices, apply_blocks(): lax.all_gather(vector, 'row', axis=0, tiled=True).reshape(-1, KB, width)  163 us
    psum x2, blocking collectives, local(): lengths = lax.psum(gram_product(moved, moved), ('sub', 'row'))  153 us
    psum x2, blocking collectives, project(): lax.psum((gram_product(current, current), gram_product(current, image_x))...  150 us
    psum x2, blocking collectives, local(): lax.psum((gram_product(basis, image_b), gram_product(basis, image_x)), 'r...  116 us
    psum x2, waiting for transfers between devices, local(): lax.psum(lax.psum((gram_product(basis, image_b), gram_product(basis, imag...  114 us
    psum x2, blocking collectives, local(): lax.psum(lax.psum((gram_product(basis, image_b), gram_product(basis, imag...  91.5 us
    psum x2, waiting for transfers between devices, local(): lax.psum((gram_product(basis, image_b), gram_product(basis, image_x)), 'r...  63.5 us
  transfers between devices with their start and end apart: 14, of which 12 were waited for; matrix products, arithmetic and copies ran while one was open for 11% of the time, Pallas kernels for 0%

profile of v1, /device:TPU:1, one launch (start us, length us, event | category | flops | bytes accessed | tf_op | source)
XLA Modules:
  0.0 1503.0 jit_solution(8680460327797210246)
XLA Ops:
  41.8 13.2 all-gather.9.cloned.1.call-done
  57.4 53.8 %reduce-scatter.13.cloned.1.call-done = f32[192,128]{1,0:T(8,128)} async-done(((f32[3072,128]{1,0:T(8,128)}), f32[192,128]{1,0:T(8,128)}) %reduce-scatter.13.cloned.1.call-update) | async-done | bytes 98320 | tf_op jit(solution)/shard_map/reduce_scatter | solution.py:71
  112.6 69.1 %all-gather.7.cloned.1.call-done = f32[12288,128]{1,0:T(8,128)} async-done(((f32[768,128]{1,0:T(8,128)}), f32[12288,128]{1,0:T(8,128)}) %all-gather.7.cloned.1.call-update) | async-done | bytes 6291472 | tf_op jit(solution)/shard_map/all_gather | solution.py:45
  192.2 78.6 %reduce-scatter.11.cloned.1.call-done = f32[768,128]{1,0:T(8,128)} async-done(((f32[12288,128]{1,0:T(8,128)}), f32[768,128]{1,0:T(8,128)}) %reduce-scatter.11.cloned.1.call-update) | async-done | bytes 393232 | tf_op jit(solution)/shard_map/reduce_scatter | solution.py:54
  277.3 76.9 %all-reduce.1 = (f32[64,64]{0,1:T(8,128)S(1)}, f32[64,64]{0,1:T(8,128)S(1)}) all-reduce(f32[64,64]{0,1:T(8,128)S(1)} %convolution_bitcast_fusion.16, f32[64,64]{0,1:T(8,128)} %fusion.130), channel_id=1, replica_groups=mesh['sub'=16,'row'=16] {'sub','row'}, use_global_device_ids=true, to_apply=%region_5.0 | all-reduce | flops 8192 | bytes 65536 | tf_op jit(solution)/shard_map/psum | solution.py:34
  411.0 21.9 %all-gather = f32[16,192,64]{1,2,0:T(8,128)} all-gather(f32[1,192,64]{1,2,0:T(8,128)S(1)} %copy.168), channel_id=1, replica_groups=mesh['sub'=16,'row'=16] {'sub'}, dimensions={0}, use_global_device_ids=true | all-gather | bytes 835584 | tf_op jit(solution)/shard_map/all_gather | solution.py:64
  441.7 45.6 %all-gather.11.cloned.1.call-done = f32[12288,64]{0,1:T(8,128)} async-done(((f32[768,64]{0,1:T(8,128)}), f32[12288,64]{0,1:T(8,128)}) %all-gather.11.cloned.1.call-update) | async-done | bytes 3145744 | tf_op jit(solution)/shard_map/all_gather | solution.py:45
  509.2 60.1 %reduce-scatter.15.cloned.1.call-done = f32[768,64]{0,1:T(8,128)} async-done(((f32[12288,64]{0,1:T(8,128)}), f32[768,64]{0,1:T(8,128)}) %reduce-scatter.15.cloned.1.call-update) | async-done | bytes 196624 | tf_op jit(solution)/shard_map/reduce_scatter | solution.py:54
  582.4 57.9 %psum.102 = f32[128,64]{0,1:T(8,128)S(1)} all-reduce(f32[128,64]{0,1:T(8,128)} %fusion.27), channel_id=1, replica_groups=mesh['sub'=16,'row'=16] {'row'}, use_global_device_ids=true, to_apply=%region_12.17 | all-reduce | flops 8192 | bytes 65536 | tf_op jit(solution)/shard_map/psum | solution.py:108
  640.2 31.4 %all-reduce.7.cloned.1.call-done = f32[128,128]{0,1:T(8,128)} async-done(((f32[128,128]{0,1:T(8,128)}), f32[128,128]{0,1:T(8,128)}) %all-reduce.7.cloned.1.call-update) | async-done | bytes 65552 | tf_op jit(solution)/shard_map/psum | solution.py:108
  671.7 45.7 %psum.103 = f32[128,64]{0,1:T(8,128)S(1)} all-reduce(f32[128,64]{0,1:T(8,128)S(1)} %psum.102), channel_id=1, replica_groups=mesh['sub'=16,'row'=16] {'sub'}, use_global_device_ids=true, to_apply=%region_13.18 | all-reduce | flops 8192 | bytes 65536 | tf_op jit(solution)/shard_map/psum | solution.py:107
  717.4 57.0 %all-reduce.9.cloned.1.call-done = f32[128,128]{0,1:T(8,128)} async-done(((f32[128,128]{0,1:T(8,128)}), f32[128,128]{0,1:T(8,128)}) %all-reduce.9.cloned.1.call-update) | async-done | bytes 65552 | tf_op jit(solution)/shard_map/psum | solution.py:107
  776.2 11.7 cholesky.127
  802.1 76.7 %psum.104 = f32[64,64]{0,1:T(8,128)S(1)} all-reduce(f32[64,64]{0,1:T(8,128)S(1)} %fusion.131), channel_id=1, replica_groups=mesh['sub'=16,'row'=16] {'sub','row'}, use_global_device_ids=true, to_apply=%region_14.21 | all-reduce | flops 4096 | bytes 32768 | tf_op jit(solution)/shard_map/psum | solution.py:115
  893.4 73.3 %all-reduce = (f32[64,64]{1,0:T(8,128)S(1)}, f32[64,64]{0,1:T(8,128)S(1)}) all-reduce(f32[64,64]{1,0:T(8,128)S(1)} %fusion.133, f32[64,64]{0,1:T(8,128)S(1)} %fusion.132), channel_id=1, replica_groups=mesh['sub'=16,'row'=16] {'sub','row'}, use_global_device_ids=true, to_apply=%region_16.24 | all-reduce | flops 8192 | bytes 65536 | tf_op jit(solution)/shard_map/psum | solution.py:34
  1019.4 20.6 %all-gather.1 = f32[16,192,64]{1,2,0:T(8,128)S(1)} all-gather(f32[1,192,64]{1,2,0:T(8,128)S(1)} %copy.198), channel_id=1, replica_groups=mesh['sub'=16,'row'=16] {'sub'}, dimensions={0}, use_global_device_ids=true | all-gather | bytes 835584 | tf_op jit(solution)/shard_map/all_gather | solution.py:64
  1047.5 48.0 %all-gather.13.cloned.1.call-done = f32[12288,64]{0,1:T(8,128)} async-done(((f32[768,64]{0,1:T(8,128)}), f32[12288,64]{0,1:T(8,128)}) %all-gather.13.cloned.1.call-update) | async-done | bytes 3145744 | tf_op jit(solution)/shard_map/all_gather | solution.py:45
  1117.5 60.4 %reduce-scatter.17.cloned.1.call-done = f32[768,64]{0,1:T(8,128)} async-done(((f32[12288,64]{0,1:T(8,128)}), f32[768,64]{0,1:T(8,128)}) %reduce-scatter.17.cloned.1.call-update) | async-done | bytes 196624 | tf_op jit(solution)/shard_map/reduce_scatter | solution.py:54
  1187.0 57.9 %psum.109 = f32[128,64]{0,1:T(8,128)S(1)} all-reduce(f32[128,64]{0,1:T(8,128)S(1)} %fusion.25), channel_id=1, replica_groups=mesh['sub'=16,'row'=16] {'row'}, use_global_device_ids=true, to_apply=%region_21.29 | all-reduce | flops 8192 | bytes 65536 | tf_op jit(solution)/shard_map/psum | solution.py:108
  1244.9 32.1 %all-reduce.11.cloned.1.call-done = f32[128,128]{0,1:T(8,128)} async-done(((f32[128,128]{0,1:T(8,128)}), f32[128,128]{0,1:T(8,128)}) %all-reduce.11.cloned.1.call-update) | async-done | bytes 65552 | tf_op jit(solution)/shard_map/psum | solution.py:108
  1277.1 45.7 %psum.110 = f32[128,64]{0,1:T(8,128)S(1)} all-reduce(f32[128,64]{0,1:T(8,128)S(1)} %psum.109), channel_id=1, replica_groups=mesh['sub'=16,'row'=16] {'sub'}, use_global_device_ids=true, to_apply=%region_22.30 | all-reduce | flops 8192 | bytes 65536 | tf_op jit(solution)/shard_map/psum | solution.py:107
  1322.8 56.7 %all-reduce.13.cloned.1.call-done = f32[128,128]{0,1:T(8,128)} async-done(((f32[128,128]{0,1:T(8,128)}), f32[128,128]{0,1:T(8,128)}) %all-reduce.13.cloned.1.call-update) | async-done | bytes 65552 | tf_op jit(solution)/shard_map/psum | solution.py:107
  1381.3 11.7 cholesky.160
  1405.3 76.7 %psum.111 = f32[64,64]{0,1:T(8,128)S(1)} all-reduce(f32[64,64]{0,1:T(8,128)S(1)} %fusion.134), channel_id=1, replica_groups=mesh['sub'=16,'row'=16] {'sub','row'}, use_global_device_ids=true, to_apply=%region_23.31 | all-reduce | flops 4096 | bytes 32768 | tf_op jit(solution)/shard_map/psum | solution.py:115
  (253 shorter events, 305.3 us)
Async XLA Ops:
  7.2 47.9 %all-gather.9.cloned.1.call-start = ((), (), s32[]{:S(2)}) async-start(), calls=%async_computation.8 | async-start | bytes 1671168 | tf_op jit(solution)/shard_map/all_gather | solution.py:64
  11.5 99.6 %reduce-scatter.13.cloned.1.call-start = ((), (), s32[]{:S(2)}) async-start(), calls=%async_computation.9 | async-start | bytes 1671168 | tf_op jit(solution)/shard_map/reduce_scatter | solution.py:71
  15.9 165.8 %all-gather.7.cloned.1.call-start = ((), (), s32[]{:S(2)}) async-start(), calls=%async_computation.6 | async-start | bytes 6684672 | tf_op jit(solution)/shard_map/all_gather | solution.py:45
  16.6 254.2 %reduce-scatter.11.cloned.1.call-start = ((), (), s32[]{:S(2)}) async-start(), calls=%async_computation.7 | async-start | bytes 6684672 | tf_op jit(solution)/shard_map/reduce_scatter | solution.py:54
  37.3 73.9 %copy-start.29 = (s32[1,1,3]{2,1,0:T(1,128)S(1)}, s32[1,1,3]{2,1,0:T(1,128)}, u32[]{:S(2)}) copy-start(s32[1,1,3]{2,1,0:T(1,128)} %param.28) | copy-start | bytes 40
  37.3 402.2 %reduce-scatter.19.cloned.1.call-start = ((), (), s32[]{:S(2)}) async-start(), calls=%async_computation.18 | async-start | bytes 1671168 | tf_op jit(solution)/shard_map/reduce_scatter | solution.py:71
  40.8 146.0 %copy-start.20 = (s32[1024]{0:T(1024)}, s32[1024]{0:T(1024)S(1)}, u32[]{:S(2)}) copy-start(s32[1024]{0:T(1024)S(1)} %pad_clamp_fusion.4) | copy-start | bytes 12292
  192.2 83.4 %copy-start.26 = (s32[1,1,12]{2,1,0:T(1,128)S(1)}, s32[1,1,12]{2,1,0:T(1,128)}, u32[]{:S(2)}) copy-start(s32[1,1,12]{2,1,0:T(1,128)} %param.29) | copy-start | bytes 148
  275.6 92.0 %copy-start.17 = (f32[768]{0:T(1024)S(1)}, f32[768]{0:T(1024)}, u32[]{:S(2)}) copy-start(f32[768]{0:T(1024)} %param.24) | copy-start | bytes 9220
  377.8 109.4 %all-gather.11.cloned.1.call-start = ((), (), s32[]{:S(2)}) async-start(), calls=%async_computation.10 | async-start | bytes 3342336 | tf_op jit(solution)/shard_map/all_gather | solution.py:45
  378.4 190.9 %reduce-scatter.15.cloned.1.call-start = ((), (), s32[]{:S(2)}) async-start(), calls=%async_computation.11 | async-start | bytes 3342336 | tf_op jit(solution)/shard_map/reduce_scatter | solution.py:54
  410.2 261.5 %all-reduce.7.cloned.1.call-start = ((), (), s32[]{:S(2)}) async-start(), calls=%async_computation.12 | async-start | bytes 131072 | tf_op jit(solution)/shard_map/psum | solution.py:108
  509.2 68.4 %copy-start.27 = (s32[1,1,12]{2,1,0:T(1,128)S(1)}, s32[1,1,12]{2,1,0:T(1,128)}, u32[]{:S(2)}) copy-start(s32[1,1,12]{2,1,0:T(1,128)} %param.29) | copy-start | bytes 148
  580.9 193.4 %all-reduce.9.cloned.1.call-start = ((), (), s32[]{:S(2)}) async-start(), calls=%async_computation.13 | async-start | bytes 131072 | tf_op jit(solution)/shard_map/psum | solution.py:107
  671.6 373.7 %reduce-scatter.21.cloned.1.call-start = ((), (), s32[]{:S(2)}) async-start(), calls=%async_computation.19 | async-start | bytes 1671168 | tf_op jit(solution)/shard_map/reduce_scatter | solution.py:71
  801.8 179.2 %copy-start.25 = (s32[1,1,12]{2,1,0:T(1,128)S(1)}, s32[1,1,12]{2,1,0:T(1,128)}, u32[]{:S(2)}) copy-start(s32[1,1,12]{2,1,0:T(1,128)} %param.30) | copy-start | bytes 148
  892.7 86.9 %copy-start.9 = (f32[768,64]{0,1:T(8,128)}, f32[768,64]{0,1:T(8,128)S(1)}, u32[]{:S(2)}) copy-start(f32[768,64]{0,1:T(8,128)S(1)} %convolution_bitcast_fusion.13) | copy-start | bytes 589828
  986.2 109.3 %all-gather.13.cloned.1.call-start = ((), (), s32[]{:S(2)}) async-start(), calls=%async_computation.14 | async-start | bytes 3342336 | tf_op jit(solution)/shard_map/all_gather | solution.py:45
  987.0 191.0 %reduce-scatter.17.cloned.1.call-start = ((), (), s32[]{:S(2)}) async-start(), calls=%async_computation.15 | async-start | bytes 3342336 | tf_op jit(solution)/shard_map/reduce_scatter | solution.py:54
  1018.5 258.5 %all-reduce.11.cloned.1.call-start = ((), (), s32[]{:S(2)}) async-start(), calls=%async_computation.16 | async-start | bytes 131072 | tf_op jit(solution)/shard_map/psum | solution.py:108
  1019.4 25.1 %copy-start.14 = (f32[768,64]{0,1:T(8,128)S(1)}, f32[768,64]{0,1:T(8,128)}, u32[]{:S(2)}) copy-start(f32[768,64]{0,1:T(8,128)} %fusion.42) | copy-start | bytes 589828
  1117.5 66.9 %copy-start.12 = (f32[12,64,64]{2,0,1:T(8,128)S(1)}, f32[12,64,64]{2,0,1:T(8,128)}, u32[]{:S(2)}) copy-start(f32[12,64,64]{2,0,1:T(8,128)} %fusion.36) | copy-start | bytes 589828
  1117.5 66.9 %copy-start.28 = (s32[1,1,12]{2,1,0:T(1,128)S(1)}, s32[1,1,12]{2,1,0:T(1,128)}, u32[]{:S(2)}) copy-start(s32[1,1,12]{2,1,0:T(1,128)} %param.29) | copy-start | bytes 148
  1186.4 193.1 %all-reduce.13.cloned.1.call-start = ((), (), s32[]{:S(2)}) async-start(), calls=%async_computation.17 | async-start | bytes 131072 | tf_op jit(solution)/shard_map/psum | solution.py:107
  (21 other events, 115.3 us)
Sparse Core Ops, SparseCore 0:
  11.7 43.3 all-gather.8
  57.6 53.5 reduce-scatter.12
  113.9 67.7 all-gather.6
  185.7 85.0 reduce-scatter.10
  377.9 52.2 reduce-scatter.18
  433.1 54.0 all-gather.10
  490.8 78.4 reduce-scatter.14
  581.0 90.5 all-reduce.6
  674.1 100.2 all-reduce.8
  986.4 52.1 reduce-scatter.20
  1041.3 54.2 all-gather.12
  1099.5 78.4 reduce-scatter.16
  1186.5 90.4 all-reduce.10
  1279.2 100.2 all-reduce.12
